TPU v7x, 32 devices: a whole 2x2x4 slice. The times are simulated.
32 devices in a mesh: dp: 8 (over y, x, core), seq: 4 (over z).
Axes of the slice: x: 2, y: 2, z: 4, core: 2. Of those that a mesh axis runs over, the one named last changes fastest.
Arguments:
- tokens: bfloat16 [32, 512, 768], P('dp', 'seq'), may hold values from -6 to 6
- segment_ids: int32 [32, 512], P('dp', 'seq'), may hold values from 0 to 7, as said below
- pair_ids: int32 [256], P('dp'), may hold values from 0 to 31
- w_qkv: bfloat16 [2, 768, 2304], replicated, may hold values from -0.21875 to 0.21875
- b_query: float32 [2, 768], replicated, may hold values from -3 to 3
- b_value: float32 [2, 768], replicated, may hold values from -3 to 3
- w_out: bfloat16 [2, 768, 768], replicated, may hold values from -0.625 to 0.625
- b_out: float32 [2, 768], replicated, may hold values from -3 to 3
- gain_one: float32 [2, 768], replicated, may hold values from 0.1 to 1.9
- shift_one: float32 [2, 768], replicated, may hold values from -3 to 3
- w_up: bfloat16 [2, 768, 3072], replicated, may hold values from -0.21875 to 0.21875
- b_up: float32 [2, 3072], replicated, may hold values from -3 to 3
- w_down: bfloat16 [2, 3072, 768], replicated, may hold values from -0.109375 to 0.109375
- b_down: float32 [2, 768], replicated, may hold values from -3 to 3
- gain_two: float32 [2, 768], replicated, may hold values from 0.1 to 1.9
- shift_two: float32 [2, 768], replicated, may hold values from -3 to 3
Outputs:
- loss: float32 [8], P('dp')
- grad_tokens: float32 [32, 512, 768], P('dp', 'seq')
- grad_w_qkv: float32 [2, 768, 2304], P(None, 'dp')
- grad_b_query: float32 [2, 768], replicated
- grad_b_value: float32 [2, 768], replicated
- grad_w_out: float32 [2, 768, 768], P(None, 'dp')
- grad_b_out: float32 [2, 768], replicated
- grad_gain_one: float32 [2, 768], replicated
- grad_shift_one: float32 [2, 768], replicated
- grad_w_up: float32 [2, 768, 3072], P(None, 'dp')
- grad_b_up: float32 [2, 3072], replicated
- grad_w_down: float32 [2, 3072, 768], P(None, 'dp')
- grad_b_down: float32 [2, 768], replicated
- grad_gain_two: float32 [2, 768], replicated
- grad_shift_two: float32 [2, 768], replicated
Inputs may be any that keep to these rules, and one draw needn't show every extreme that they name: `segment_ids`: each row holds exactly 8 segments, numbered 0 to 7 in order of position, each of one or more tokens. The partner of segment i of index g of dp is the segment of number pair_ids[i] among the 32 segments of the same g.
All inputs are finite; a program needn't handle non-finite values.
Results may differ from a plain program's by a relative error of at most 0.02.
Values may be sent and summed in bfloat16 or wider, within the bound.
A program may use at most 256 MiB of HBM per device.

v0:
```python
import functools

import jax
import jax.numpy as jnp
from jax import lax
from jax.experimental import pallas as pl
from jax.experimental.pallas import tpu as pltpu
from jax.sharding import PartitionSpec as P

MESH = pl.DeviceIdType.MESH
LOSS_SCALE = 1024.0
NORM_EPS = 1e-06
HD = 64
WIDE = 768
C = 256
WAYS = 8
QUEUE = 18
SLOTS = 6
LAGS = (0, 1, 3, 5, 7, 9, 11)
PACE = (5, 6)
GT_PARTS = 4
VEC_ROWS = 16


def dot(left, right):
    return lax.dot_general(
        left,
        right,
        (((1,), (0,)), ((), ())),
        preferred_element_type=jnp.float32,
    )


def dot_t(left, right):
    return lax.dot_general(
        left,
        right,
        (((1,), (1,)), ((), ())),
        preferred_element_type=jnp.float32,
    )


def split(values):
    high = values.astype(jnp.bfloat16)
    return high, (values - high.astype(jnp.float32)).astype(jnp.bfloat16)


def remote(src, dst, send_sem, recv_sem, where):
    return pltpu.make_async_remote_copy(
        src_ref=src,
        dst_ref=dst,
        send_sem=send_sem,
        recv_sem=recv_sem,
        device_id=where,
        device_id_type=MESH,
    )


def greet(peers):
    barrier = pltpu.get_barrier_semaphore()
    for peer in peers:
        pl.semaphore_signal(barrier, inc=1, device_id=peer, device_id_type=MESH)
    pl.semaphore_wait(barrier, len(peers))


def gelu_pair(x):
    t = 1.0 / (1.0 + 0.23164190 * jnp.abs(x))
    gauss = jnp.exp(-0.5 * x * x)
    poly = t * (
        0.127414796
        + t * (-0.142248368 + t * (0.7107068705 + t * (-0.7265760135 + t * 0.5307027145)))
    )
    tail = poly * gauss
    phi = jnp.where(x >= 0.0, 1.0 - tail, tail)
    return x * phi, phi + x * (gauss * 0.3989422804014327)


def norm(x, gain, shift):
    centre = x - jnp.mean(x, axis=-1, keepdims=True)
    scaled = lax.rsqrt(jnp.mean(centre * centre, axis=-1, keepdims=True) + NORM_EPS)
    normal = centre * scaled
    return normal * gain + shift, normal, scaled


def fwd_kernel(
    layers, segs,
    tok, ids, pair, b_query, b_value, b_out, gain_one, shift_one, b_up, b_down, gain_two, shift_two,
    w_qkv, w_out, w_up, w_down,
    grad_out, loss_out, o_qkv, o_p, o_rl, o_pv, o_hidT, o_mixT, o_nrmT, o_actT, o_gp, o_n1, o_r1, o_n2, o_r2,
    wq, wo, wu, wd, bias, hid, low, idbuf, qkv, pb, rl, pv, mix, nrm, gp, n1, r1, n2, r2,
    hidT, mixT, nrmT, actT, acc, ubuf, gbuf, prow,
    wsem, osem, tsem, usem,
):
    T, D = hid.shape
    FF = w_up.shape[2]
    piece = tok.shape[1]
    parts = T // piece
    me = lax.axis_index("dp")
    zi = lax.axis_index("seq")
    pairs = ((w_qkv, wq), (w_out, wo), (w_up, wu), (w_down, wd))

    def wcopy(l, i):
        return pltpu.make_async_copy(pairs[i][0].at[l], pairs[i][1], wsem.at[i])

    def peer(k):
        return lax.rem(zi + k, parts)

    mine = pl.ds(pl.multiple_of(zi * piece, piece), piece)

    def tcopy(k, n):
        src, dst = ((tok, low.at[mine]), (ids, idbuf.at[zi]))[n]
        if k == 0:
            return pltpu.make_async_copy(src.at[zi], dst, tsem.at[n, 0, 0])
        return remote(src.at[peer(k)], dst, tsem.at[n, 0, k], tsem.at[n, 1, k], (me, peer(k)))

    greet([(me, peer(k)) for k in range(1, parts)])
    for k in (2, 1, 3, 0):
        for n in (1, 0):
            tcopy(k, n).start()
    for i in range(4):
        wcopy(0, i).start()

    def refill(l, *which):
        @pl.when(l + 1 < layers)
        def _():
            for i in which:
                wcopy(l + 1, i).start()

    lane = lax.broadcasted_iota(jnp.int32, (T, 128), 1)
    first = lane < HD

    homes = (
        (qkv, o_qkv), (hidT, o_hidT), (rl, o_rl), (pv, o_pv), (mixT, o_mixT), (n1, o_n1), (r1, o_r1),
        (nrmT, o_nrmT), (gp, o_gp), (actT, o_actT), (n2, o_n2), (r2, o_r2), (pb, o_p),
    )

    def home(l, k):
        return pltpu.make_async_copy(homes[k][0], homes[k][1].at[l], osem.at[k])

    def ship(l, *keys):
        for k in keys:
            home(l, k).start()

    def claim(l, *keys):
        @pl.when(l > 0)
        def _():
            for k in keys:
                home(l - 1, k).wait()

    for k in range(parts):
        tcopy(k, 1).wait()
    id_rows = [idbuf[k] for k in range(parts)]
    id_cols = jnp.concatenate(
        id_rows + [jnp.zeros((8 - parts, piece), jnp.int32)], axis=0
    ).astype(jnp.float32).T
    for i in range(parts):
        for j in range(parts):
            same = id_cols[:, i : i + 1] == id_rows[j].astype(jnp.float32)
            bias[i * piece : (i + 1) * piece, j * piece : (j + 1) * piece] = jnp.where(same, 0.0, -1e30)
    for k in (0, 1, 3, 2):
        tcopy(k, 0).wait()
        source = pl.ds(pl.multiple_of(lax.rem(zi + parts - k, parts) * piece, piece), piece)
        arrived = low[source, :]
        hid[source, :] = arrived.astype(jnp.float32)
        hidT[:, source] = arrived.T

    def layer(l, carry):
        row = pl.ds(l, 1)
        wcopy(l, 0).wait()
        y = dot(low[...], wq[...])
        refill(l, 0)
        claim(l, 0)
        qkv[:, :D] = ((y[:, :D] + b_query[row, :]) * 0.125).astype(jnp.bfloat16)
        qkv[:, D : 2 * D] = y[:, D : 2 * D].astype(jnp.bfloat16)
        qkv[:, 2 * D :] = (y[:, 2 * D :] + b_value[row, :]).astype(jnp.bfloat16)
        ship(l, 0)
        ship(l, 1)

        def scores(n):
            o = n // 2 * 128
            q2 = qkv[:, o : o + 128]
            sel = first if n % 2 == 0 else ~first
            return dot_t(jnp.where(sel, q2, jnp.zeros_like(q2)), qkv[:, D + o : D + o + 128]) + bias[...]

        claim(l, 2, 3, 4, 12)
        made = {0: scores(0)}
        for n in range(D // HD):
            if n + 1 < D // HD:
                made[n + 1] = scores(n + 1)
            cols = slice(n // 2 * 128, n // 2 * 128 + 128)
            v2 = qkv[:, 2 * D + cols.start : 2 * D + cols.stop]
            sel = first if n % 2 == 0 else ~first
            sc = made.pop(n)
            e = jnp.exp(sc - jnp.max(sc, axis=-1, keepdims=True))
            recip = 1.0 / jnp.sum(e, axis=-1, keepdims=True)
            p = e.astype(jnp.bfloat16)
            pb[n] = p
            part = dot(p, jnp.where(sel, v2, jnp.zeros_like(v2))) * recip
            if n % 2 == 0:
                total, before = part, recip
                continue
            total = total + part
            rl[:, cols] = jnp.where(first, before, recip)
            pv[:, cols] = total
            low_total = total.astype(jnp.bfloat16)
            mix[:, cols] = low_total
            mixT[cols, :] = low_total.T
        ship(l, 12)
        ship(l, 2)
        ship(l, 3)
        wcopy(l, 1).wait()
        acc[...] = dot(mix[...], wo[...])
        refill(l, 1)
        ship(l, 4)

        claim(l, 5, 6, 7)
        x = hid[...] + acc[...] + b_out[row, :]
        y, n, r = norm(x, gain_one[row, :], shift_one[row, :])
        nrm[...] = y
        rounded = y.astype(jnp.bfloat16)
        low[...] = rounded
        nrmT[...] = rounded.T
        n1[...] = n.astype(jnp.bfloat16)
        r1[...] = jnp.broadcast_to(r, (T, 128))
        ship(l, 5)
        ship(l, 6)
        ship(l, 7)
        wcopy(l, 2).wait()
        wcopy(l, 3).wait()
        acc[...] = nrm[...]
        claim(l, 8, 9)

        def raised(j):
            cols = slice(j * WIDE, (j + 1) * WIDE)
            return dot(low[...], wu[:, cols]) + b_up[row, cols]

        made = {0: raised(0)}
        for j in range(FF // WIDE):
            cols = slice(j * WIDE, (j + 1) * WIDE)
            if j + 1 < FF // WIDE:
                made[j + 1] = raised(j + 1)
            a, g = gelu_pair(made.pop(j))
            al = a.astype(jnp.bfloat16)
            gp[:, cols] = g.astype(jnp.bfloat16)
            actT[cols, :] = al.T
            acc[...] += dot(al, wd[cols, :])
        refill(l, 2, 3)
        ship(l, 8)
        ship(l, 9)

        claim(l, 10, 11)
        home(l, 1).wait()
        x = acc[...] + b_down[row, :]
        y, n, r = norm(x, gain_two[row, :], shift_two[row, :])
        hid[...] = y

        @pl.when(l + 1 < layers)
        def _():
            rounded = hid[...].astype(jnp.bfloat16)
            low[...] = rounded
            hidT[...] = rounded.T

        n2[...] = n.astype(jnp.bfloat16)
        r2[...] = jnp.broadcast_to(r, (T, 128))
        ship(l, 10)
        ship(l, 11)
        return carry

    lax.fori_loop(0, layers, layer, 0)

    count = parts * segs
    member_t = jnp.concatenate(
        [
            (lax.broadcasted_iota(jnp.int32, (segs, piece), 0) == row).astype(jnp.float32)
            for row in id_rows
        ],
        axis=1,
    )
    sizes = jnp.sum(member_t, axis=-1, keepdims=True)
    member_t = member_t.astype(jnp.bfloat16)
    high, rest = split(hid[...])
    embed = (dot(member_t, high) + dot(member_t, rest)) / sizes
    scale = lax.rsqrt(jnp.sum(embed * embed, axis=-1, keepdims=True) + NORM_EPS)
    unit = embed * scale
    ubuf[...] = jnp.zeros_like(ubuf)
    gbuf[zi] = unit

    def ucopy(k):
        return remote(gbuf.at[zi], gbuf.at[zi], usem.at[0, k], usem.at[1, k], (me, peer(k)))

    for k in range(1, parts):
        ucopy(k).start()
    prow[...] = jnp.zeros_like(prow)
    prow[:1, :count] = pair[...].astype(jnp.float32)
    partner = prow[...].T[:, :1]
    side = ubuf.shape[0]
    row_no = lax.broadcasted_iota(jnp.int32, (side, side), 0)
    col_no = lax.broadcasted_iota(jnp.int32, (side, side), 1)
    live = (row_no < count) & (col_no < count)
    chosen = jnp.where(live & (partner == col_no.astype(jnp.float32)), 1.0, 0.0)
    for k in range(1, parts):
        ucopy(k).wait()
    for k in range(parts):
        ubuf[k * segs : (k + 1) * segs, :] = gbuf[k]
    high, rest = split(ubuf[...])
    logits = 20.0 * (dot_t(high, high) + dot_t(high, rest) + dot_t(rest, high))
    logits = jnp.where(live, logits, -1e30)
    top = jnp.max(logits, axis=-1, keepdims=True)
    grown = jnp.exp(logits - top)
    total = jnp.sum(grown, axis=-1, keepdims=True)
    pull = jnp.where(live, (grown / total - chosen) * (20.0 * LOSS_SCALE / count), 0.0)
    acc[:side, :side] = pull + pull.T
    own = pl.ds(pl.multiple_of(zi * segs, segs), segs)
    ours, ours_rest = split(acc[own, :side])
    grad_unit = dot(ours, high) + dot(ours, rest) + dot(ours_rest, high)
    inner = jnp.sum(grad_unit * unit, axis=-1, keepdims=True)
    grad_sums = scale * (grad_unit - unit * inner) / sizes
    high, rest = split(grad_sums)
    both = jnp.concatenate([grad_sums, grad_sums - high.astype(jnp.float32)], axis=0).astype(jnp.bfloat16)
    lanes = lax.broadcasted_iota(jnp.int32, (piece, 2 * segs), 1)
    lanes = jnp.where(lanes < segs, lanes, lanes - segs).astype(jnp.float32)
    for i in range(parts):
        member = (lanes == id_cols[:, i : i + 1]).astype(jnp.bfloat16)
        grad_out[i * piece : (i + 1) * piece, :] = dot(member, both)
    picked = jnp.sum(chosen * logits, axis=-1, keepdims=True)
    losses = jnp.where(row_no[:, :1] < count, top + jnp.log(total) - picked, 0.0)
    loss_out[...] = jnp.sum(losses, axis=0, keepdims=True) / count
    for k in range(len(homes)):
        if k != 1:
            home(layers - 1, k).wait()


def forward(tokens, segment_ids, pair_ids, w):
    parts, piece, D = tokens.shape
    T = parts * piece
    L = w["w_qkv"].shape[0]
    FF = w["w_up"].shape[2]
    segs = pair_ids.shape[0] // parts
    side = 128
    bf, f32 = jnp.bfloat16, jnp.float32
    S = jax.ShapeDtypeStruct
    V = pltpu.VMEM
    vm = pl.BlockSpec(memory_space=V)
    anyspec = pl.BlockSpec(memory_space=pl.ANY)
    H = D // HD
    dma = pltpu.SemaphoreType.DMA
    out_shape = (
        S((T, D), f32), S((1, 1), f32), S((L, T, 3 * D), bf), S((L, H, T, T), bf), S((L, T, D), f32), S((L, T, D), f32),
        S((L, D, T), bf), S((L, D, T), bf), S((L, D, T), bf), S((L, FF, T), bf), S((L, T, FF), bf),
        S((L, T, D), bf), S((L, T, 128), f32), S((L, T, D), bf), S((L, T, 128), f32),
    )
    scratch = [
        V((D, 3 * D), bf), V((D, D), bf), V((D, FF), bf), V((FF, D), bf),
        V((T, T), f32), V((T, D), f32), V((T, D), bf), V((parts, 1, piece), jnp.int32),
        V((T, 3 * D), bf), V((H, T, T), bf), V((T, D), f32), V((T, D), f32), V((T, D), bf), V((T, D), f32), V((T, FF), bf),
        V((T, D), bf), V((T, 128), f32), V((T, D), bf), V((T, 128), f32),
        V((D, T), bf), V((D, T), bf), V((D, T), bf), V((FF, T), bf), V((T, D), f32),
        V((side, D), f32), V((parts, segs, D), f32), V((8, side), f32),
        dma((4,)), dma((13,)), dma((2, 2, parts)), dma((2, parts)),
    ]
    return pl.pallas_call(
        functools.partial(fwd_kernel, L, segs),
        out_shape=out_shape,
        in_specs=[anyspec] * 2 + [vm] * 10 + [anyspec] * 4,
        out_specs=(vm, vm) + (anyspec,) * 13,
        scratch_shapes=scratch,
        compiler_params=pltpu.CompilerParams(
            vmem_limit_bytes=60 * 1024 * 1024, collective_id=1, has_side_effects=True
        ),
        name="forward",
    )(
        tokens, segment_ids.reshape(parts, 1, piece), pair_ids.reshape(1, -1),
        *(w[k] for k in ("b_query", "b_value", "b_out", "gain_one", "shift_one", "b_up", "b_down", "gain_two", "shift_two")),
        *(w[k] for k in ("w_qkv", "w_out", "w_up", "w_down")),
    )


def low_sum(one, other):
    return one + other


def bwd_kernel(
    layers, g_in, gain_one, gain_two,
    w_qkv, w_out, w_up, w_down,
    h_qkv, h_p, h_rl, h_pv, h_hidT, h_mixT, h_nrmT, h_actT, h_gp, h_n1, h_r1, h_n2, h_r2,
    out, gt_out, vec_out,
    wd, wu, gp, actT, wq, qkv, pb, rl, pv, wo, hidT, mixT, nrmT, n1, r1, n2, r2,
    acc, second, branch, gm, gpre, rhs, vec, vrecv, gb,
    sendc, keepq, recvq, s1, k1, t1, s2, k2, t2, za, zr, zb, zt, zf,
    fsem, asem, lsem, csem, xsem, ysem, zsem, osem, vsem, gsem,
):
    T, D = g_in.shape
    FF = w_up.shape[2]
    R = D // WAYS
    U = 4 * R
    n_ffn = FF // D
    n_att = D // 128
    group = D // C
    macros = n_ffn + n_att
    per = n_ffn * group + n_att
    n_units = layers * per
    n_macros = layers * macros

    me = lax.axis_index("dp")
    zi = lax.axis_index("seq")
    oc = lax.rem(me, 2)
    ox = lax.rem(lax.div(me, 2), 2)
    oy = lax.rem(lax.div(me, 4), 2)
    core = (me + 1 - 2 * oc, zi)
    xdev = (me + 2 - 4 * ox, zi)
    ydev = (me + 4 - 8 * oy, zi)
    inner = (zi == 1) | (zi == 2)
    outer = (zi == 0) | (zi == 3)
    to_inner = (me, 1 + lax.div(zi, 2))
    across = (me, 3 - zi)
    to_outer = (me, 3 * lax.div(zi, 2))

    def place(n):
        y = lax.rem(oy + n // 2 % 2, 2)
        x = lax.rem(ox + n % 2, 2)
        return 4 * y + 2 * x + lax.rem(oc + n // 4, 2)

    def turned(src, dst, l):
        return [(src.at[l, place(n)], dst.at[pl.ds(n * R, R)]) for n in range(WAYS)]

    def copies(parts, sem):
        return [pltpu.make_async_copy(a, b, sem.at[k]) for k, (a, b) in enumerate(parts)]

    def ffn_tile(f):
        l = layers - 1 - lax.div(f, n_ffn)
        rb = lax.rem(f, n_ffn)
        s = lax.rem(f, 2)
        span = pl.ds(pl.multiple_of(rb * D, D), D)
        parts = [(w_down.at[l, span], wd.at[s]), (w_up.at[l, :, span], wu.at[s]), (h_gp.at[l, :, span], gp.at[s])]
        parts += [(h_actT.at[l, place(n), rb], actT.at[s, pl.ds(n * R, R)]) for n in range(WAYS)]
        return copies(parts, fsem.at[s])

    def att_tile(a):
        l = layers - 1 - lax.div(a, n_att)
        i = lax.rem(a, n_att)
        s = lax.rem(a, 2)
        parts = [(h_p.at[l, pl.ds(2 * i, 2)], pb.at[s])]
        for k in range(3):
            span = pl.ds(pl.multiple_of(i * 128 + k * D, 128), 128)
            parts.append((w_qkv.at[l, :, span], wq.at[s, :, pl.ds(k * 128, 128)]))
            parts.append((h_qkv.at[l, :, span], qkv.at[s, :, pl.ds(k * 128, 128)]))
        span = pl.ds(pl.multiple_of(i * 128, 128), 128)
        parts += [(h_rl.at[l, :, span], rl.at[s]), (h_pv.at[l, :, span], pv.at[s])]
        return copies(parts, asem.at[s])

    def ffn_layer(l):
        return copies([(h_n2.at[l], n2), (h_r2.at[l], r2)] + turned(h_nrmT, nrmT, l), lsem.at[0])

    def att_layer(l):
        parts = [(h_n1.at[l], n1), (h_r1.at[l], r1), (w_out.at[l], wo)]
        return copies(parts + turned(h_hidT, hidT, l) + turned(h_mixT, mixT, l), lsem.at[1])

    def start(made):
        for c in made:
            c.start()

    def wait(made):
        for c in made:
            c.wait()

    start(ffn_layer(layers - 1))
    for n in range(2):
        start(ffn_tile(jnp.int32(n)))
    start(att_layer(layers - 1))
    for n in range(2):
        start(att_tile(jnp.int32(n)))
    acc[...] = g_in[...]
    vec[...] = jnp.zeros_like(vec)
    greet([core, xdev, ydev] + [(me, lax.rem(zi + k, 4)) for k in range(1, 4)])

    lane = lax.broadcasted_iota(jnp.int32, (T, 128), 1)
    first = lane < HD

    def norm_back(g, n, r, gain):
        e = g * gain
        return r * (e - jnp.mean(e, axis=-1, keepdims=True) - n * jnp.mean(e * n, axis=-1, keepdims=True))

    def col_sum(v):
        return jnp.sum(v.astype(jnp.float32), axis=0, keepdims=True)

    def through_norm(l, base, normal, root, gain, rounded):
        g = acc[...]
        n = normal[...].astype(jnp.float32)
        d = norm_back(g, n, root[:, :1], gain)
        acc[...] = d
        low = d.astype(jnp.bfloat16)
        rounded[...] = low
        for k, v in enumerate((low, g * n, g)):
            vec[l, base + k : base + k + 1, :] = col_sum(v)

    def prologue(l):
        wait(ffn_layer(l))
        through_norm(l, 5 + n_ffn, n2, r2, gain_two[pl.ds(l, 1), :], second)

    def middle(l):
        wait(att_layer(l))
        through_norm(l, 2, n1, r1, gain_one[pl.ds(l, 1), :], branch)
        gm[...] = dot_t(branch[...], wo[...]).astype(jnp.bfloat16)

    def ffn(l, rb, c):
        f = (layers - 1 - l) * n_ffn + rb
        s = lax.rem(f, 2)
        q = rb * group
        wait(ffn_tile(f))
        low = (dot_t(second[...], wd[s]) * gp[s].astype(jnp.float32)).astype(jnp.bfloat16)
        gpre[...] = low
        vec[l, pl.ds(5 + rb, 1), :] = col_sum(low)
        for k, (left, right) in enumerate(((nrmT, gpre), (actT.at[s], second))):
            made = dot(left[...], right[...]).astype(jnp.bfloat16)
            for n in range(group):
                keepq[q + n, k] = made[:U, n * C : (n + 1) * C]
                sendc[c, n, k] = made[U:, n * C : (n + 1) * C]
        acc[...] += dot_t(gpre[...], wu[s])

        @pl.when(f + 2 < layers * n_ffn)
        def _():
            start(ffn_tile(f + 2))

    def attend(l, i, c):
        a = (layers - 1 - l) * n_att + i
        o = pl.multiple_of(i * 128, 128)
        s = lax.rem(a, 2)
        q = n_ffn * group + i
        wait(att_tile(a))
        q2, k2, v2 = (qkv[s, :, k * 128 : (k + 1) * 128] for k in range(3))
        g2 = (gm[:, pl.ds(o, 128)].astype(jnp.float32) * rl[s]).astype(jnp.bfloat16)
        weighed = g2.astype(jnp.float32) * pv[s]
        zero = jnp.zeros_like(q2)
        q2t, g2t = q2.T, g2.T
        dq = None
        dkt, dvt = [], []
        for h in range(2):
            sel = first if h == 0 else ~first
            p = pb[s, h]
            gprob = dot_t(jnp.where(sel, g2, zero), v2)
            centre = jnp.sum(jnp.where(sel, weighed, 0.0), axis=-1, keepdims=True)
            ds = (p.astype(jnp.float32) * (gprob - centre)).astype(jnp.bfloat16)
            part = dot(ds, jnp.where(sel, k2, zero))
            dq = part if h == 0 else dq + part
            dkt.append(dot(q2t[h * HD : (h + 1) * HD], ds))
            dvt.append(dot(g2t[h * HD : (h + 1) * HD], p))
        dq = (dq * 0.125).astype(jnp.bfloat16)
        dk = jnp.concatenate(dkt, axis=0).astype(jnp.bfloat16).T
        dv = jnp.concatenate(dvt, axis=0).astype(jnp.bfloat16).T
        vec[l, 0:1, pl.ds(o, 128)] = col_sum(dq)
        vec[l, 1:2, pl.ds(o, 128)] = col_sum(dv)
        rhs[:, :128] = dq
        rhs[:, 128:256] = dk
        rhs[:, 256:] = dv
        made = dot(hidT[...], rhs[...]).astype(jnp.bfloat16)
        keepq[q, 0] = made[:U, :C]
        sendc[c, 0, 0] = made[U:, :C]
        keepq[q, 1, :, :128] = made[:U, C:]
        sendc[c, 0, 1, :, :128] = made[U:, C:]
        made = dot(mixT[...], branch[:, pl.ds(o, 128)]).astype(jnp.bfloat16)
        keepq[q, 1, :, 128:] = made[:U]
        sendc[c, 0, 1, :, 128:] = made[U:]
        acc[...] += dot_t(rhs[...], wq[s])

        @pl.when(a + 2 < layers * n_att)
        def _():
            start(att_tile(a + 2))

    def core_copy(m, wide):
        c = lax.rem(m, 2)
        k = lax.rem(m, macros)
        q = k * group if wide else n_ffn * group + k - n_ffn
        size = group if wide else 1
        return remote(
            sendc.at[c, pl.ds(0, size)], recvq.at[pl.ds(q, size)], csem.at[0, m], csem.at[1, m], core
        )

    def is_wide(m):
        return lax.rem(m, macros) < n_ffn

    def copies_one(u):
        s = lax.rem(u, SLOTS)
        return [
            remote(s1.at[s, k], t1.at[s, k], xsem.at[0, k, s], xsem.at[1, k, s], (xdev, ydev)[k]) for k in range(2)
        ]

    def copy_two(u, k):
        s = lax.rem(u, SLOTS)
        return remote(s2.at[s, k], t2.at[s, k], ysem.at[0, k, s], ysem.at[1, k, s], (ydev, xdev)[k])

    def copy_in(u, k):
        s = lax.rem(u, SLOTS)
        return remote(za.at[s, k], zr.at[s, k], zsem.at[0, k, s], zsem.at[1, k, s], to_inner)

    def copy_across(u, k):
        s = lax.rem(u, SLOTS)
        return remote(zb.at[s, k], zt.at[s, k], zsem.at[2, k, s], zsem.at[3, k, s], across)

    def copy_out(u, k):
        s = lax.rem(u, SLOTS)
        return remote(zf.at[s, k], out.at[u, k], zsem.at[4, k, s], zsem.at[5, k, s], to_outer)

    def copy_home(u):
        s = lax.rem(u, SLOTS)
        return pltpu.make_async_copy(zf.at[s], out.at[u], osem.at[s])

    def stage_one(u):
        s = lax.rem(u, QUEUE)
        d = lax.rem(u, SLOTS)
        base = lax.div(u, per) * macros

        @pl.when(u == 0)
        def _():
            core_copy(base, True).wait_recv()

        @pl.when(u >= n_units - 2)
        def _():
            core_copy(base + n_ffn + s - n_ffn * group, False).wait_recv()

        for k in range(2):
            sent, kept = ((1, 3), (0, 2)) if k == 0 else ((2, 3), (0, 1))
            for n, (a, b) in enumerate(zip(sent, kept)):
                to = pl.ds(n * R, R)
                s1[d, k, to] = low_sum(keepq[s, k, pl.ds(a * R, R)], recvq[s, k, pl.ds(a * R, R)])
                k1[d, k, to] = low_sum(keepq[s, k, pl.ds(b * R, R)], recvq[s, k, pl.ds(b * R, R)])
        start(copies_one(u))

    def stage_two(u):
        d = lax.rem(u, SLOTS)
        wait(copies_one(u))
        for k in range(2):
            s2[d, k] = low_sum(k1[d, k, pl.ds(R, R)], t1[d, k, pl.ds(R, R)])
            k2[d, k] = low_sum(k1[d, k, pl.ds(0, R)], t1[d, k, pl.ds(0, R)])
        start([copy_two(u, k) for k in range(2)])

    def stage_three(u):
        d = lax.rem(u, SLOTS)
        for k in range(2):
            copy_two(u, k).wait()
            za[d, k] = low_sum(k2[d, k], t2[d, k])

            @pl.when(outer)
            def _(k=k):
                copy_in(u, k).start()

    def stage_four(u):
        d = lax.rem(u, SLOTS)

        @pl.when(outer)
        def _():
            for k in range(2):
                copy_in(u, k).wait_send()

        @pl.when(inner)
        def _():
            for k in range(2):
                copy_in(u, k).wait_recv()
                zb[d, k] = low_sum(za[d, k], zr[d, k])
                copy_across(u, k).start()

    def stage_five(u):
        d = lax.rem(u, SLOTS)

        @pl.when(inner)
        def _():
            for k in range(2):
                copy_across(u, k).wait()
                zf[d, k] = low_sum(zb[d, k], zt[d, k])
                copy_out(u, k).start()
            copy_home(u).start()

    def stage_six(u):
        @pl.when(inner)
        def _():
            for k in range(2):
                copy_out(u, k).wait_send()
            copy_home(u).wait()

        @pl.when(outer)
        def _():
            for k in range(2):
                copy_out(u, k).wait_recv()

    stages = (None, stage_one, stage_two, stage_three, stage_four, stage_five, stage_six)

    def run_stage(i, k):
        u = i - LAGS[k]

        @pl.when((u >= 0) & (u < n_units))
        def _():
            stages[k](u)

    def vec_copy(k):
        where = (core, xdev, ydev, to_inner, across, to_outer)[k]
        return remote(vec, vrecv.at[k], vsem.at[0, k], vsem.at[1, k], where)

    def vec_step(k):
        if 1 <= k <= 3:
            vec_copy(k - 1).wait()
            vec[...] += vrecv[k - 1]
        if k < 3:
            vec_copy(k).start()
        if k == 3:

            @pl.when(outer)
            def _():
                vec_copy(3).start()

        if k == 4:

            @pl.when(outer)
            def _():
                vec_copy(3).wait_send()

            @pl.when(inner)
            def _():
                vec_copy(3).wait_recv()
                vec[...] += vrecv[3]
                vec_copy(4).start()

        if k == 5:

            @pl.when(inner)
            def _():
                vec_copy(4).wait()
                vec[...] += vrecv[4]
                vec_copy(5).start()

        if k == 6:

            @pl.when(inner)
            def _():
                vec_copy(5).wait_send()
                vec_out[...] = vec[...]

            @pl.when(outer)
            def _():
                vec_copy(5).wait_recv()
                vec_out[...] = vrecv[5]

    part = T // 4
    slab = part // GT_PARTS

    def gt_own():
        own = pl.ds(pl.multiple_of(zi * part, part), part)
        return pltpu.make_async_copy(gb.at[own], gt_out.at[zi], gsem.at[0, 3 * GT_PARTS])

    def gt_copy(n):
        peer = lax.rem(zi + 1 + lax.rem(n, 3), 4)
        o = lax.div(n, 3) * slab
        src = gb.at[pl.ds(pl.multiple_of(peer * part + o, slab), slab)]
        dst = gt_out.at[zi, pl.ds(pl.multiple_of(o, slab), slab)]
        return remote(src, dst, gsem.at[0, n], gsem.at[1, n], (me, peer))

    def done_by(i):
        num, den = PACE
        return jnp.minimum(lax.div(num * (i + 1) + den - 1, den), n_macros)

    last = 0
    while -(-PACE[0] * (last + 1) // PACE[1]) < n_macros:
        last += 1

    def step(i, carry):
        for k in range(6, 1, -1):
            run_stage(i, k)
        run_stage(i, 1)
        m = done_by(i - 1)
        l = layers - 1 - lax.div(m, macros)
        k = lax.rem(m, macros)
        c = lax.rem(m, 2)
        busy = done_by(i) > m

        @pl.when(busy & (m >= 2) & is_wide(m - 2))
        def _():
            core_copy(m - 2, True).wait_send()

        @pl.when(busy & (m >= 3) & is_wide(m - 2))
        def _():
            core_copy(m - 2, True).wait_recv()

        @pl.when(busy & (m >= 2) & ~is_wide(m - 2))
        def _():
            core_copy(m - 2, False).wait()

        @pl.when(busy & (k == 0))
        def _():
            prologue(l)

        @pl.when(busy & (k == 0) & (l < layers - 1))
        def _():
            start(att_layer(l))

        @pl.when(busy & (k < n_ffn))
        def _():
            ffn(l, k, c)
            core_copy(m, True).start()

        @pl.when(busy & (k == n_ffn) & (l > 0))
        def _():
            start(ffn_layer(l - 1))

        @pl.when(busy & (k == n_ffn))
        def _():
            middle(l)

        @pl.when(busy & (k >= n_ffn))
        def _():
            attend(l, k - n_ffn, c)
            core_copy(m, False).start()

        @pl.when(i == last + 1)
        def _():
            gb[...] = acc[...].astype(jnp.bfloat16)
            gt_own().start()

        @pl.when((i > last) & (i <= last + 3 * GT_PARTS))
        def _():
            gt_copy(i - last - 1).start()

        for n in range(7):

            @pl.when(i == last + 1 + 2 * n)
            def _(n=n):
                vec_step(n)

        return carry

    lax.fori_loop(0, n_units + LAGS[6], step, 0)
    for m in (n_macros - 2, n_macros - 1):
        core_copy(jnp.int32(m), False).wait_send()
    gt_own().wait()

    def gt_wait(n, c):
        gt_copy(n).wait()
        return c

    lax.fori_loop(0, 3 * GT_PARTS, gt_wait, 0)


def backward(grad_hidden, res, w):
    T, D = grad_hidden.shape
    L = w["w_qkv"].shape[0]
    FF = w["w_up"].shape[2]
    bf, f32 = jnp.bfloat16, jnp.float32
    S = jax.ShapeDtypeStruct
    V = pltpu.VMEM
    vm = pl.BlockSpec(memory_space=V)
    anyspec = pl.BlockSpec(memory_space=pl.ANY)
    R = D // WAYS
    U = 4 * R
    group = D // C
    n_units = L * (FF // C + D // 128)
    n_macros = L * (FF // D + D // 128)
    dma = pltpu.SemaphoreType.DMA
    scratch = [
        V((2, D, D), bf), V((2, D, D), bf), V((2, T, D), bf), V((2, D, T), bf),
        V((2, D, 384), bf), V((2, T, 384), bf), V((2, 2, T, T), bf), V((2, T, 128), f32), V((2, T, 128), f32),
        V((D, D), bf), V((D, T), bf), V((D, T), bf), V((D, T), bf),
        V((T, D), bf), V((T, 128), f32), V((T, D), bf), V((T, 128), f32),
        V((T, D), f32), V((T, D), bf), V((T, D), bf), V((T, D), bf), V((T, D), bf), V((T, 384), bf),
        V((L, VEC_ROWS, D), f32), V((6, L, VEC_ROWS, D), f32), V((T, D), bf),
        V((2, group, 2, U, C), bf), V((QUEUE, 2, U, C), bf), V((QUEUE, 2, U, C), bf),
        V((SLOTS, 2, 2 * R, C), bf), V((SLOTS, 2, 2 * R, C), bf), V((SLOTS, 2, 2 * R, C), bf),
        V((SLOTS, 2, R, C), bf), V((SLOTS, 2, R, C), bf), V((SLOTS, 2, R, C), bf),
        V((SLOTS, 2, R, C), bf), V((SLOTS, 2, R, C), bf), V((SLOTS, 2, R, C), bf),
        V((SLOTS, 2, R, C), bf), V((SLOTS, 2, R, C), bf),
        dma((2, 3 + WAYS)), dma((2, 9)), dma((2, 3 + 2 * WAYS)), dma((2, n_macros)), dma((2, 2, SLOTS)), dma((2, 2, SLOTS)),
        dma((6, 2, SLOTS)), dma((SLOTS,)), dma((2, 6)), dma((2, 3 * GT_PARTS + 1)),
    ]
    return pl.pallas_call(
        functools.partial(bwd_kernel, L),
        out_shape=(
            S((n_units, 2, R, C), bf), S((4, T // 4, D), bf), S((L, VEC_ROWS, D), f32),
        ),
        in_specs=[vm] * 3 + [anyspec] * 17,
        out_specs=(anyspec, anyspec, vm),
        scratch_shapes=scratch,
        compiler_params=pltpu.CompilerParams(
            vmem_limit_bytes=60 * 1024 * 1024, collective_id=0, has_side_effects=True
        ),
        name="backward",
    )(
        grad_hidden, w["gain_one"], w["gain_two"],
        *(w[k] for k in ("w_qkv", "w_out", "w_up", "w_down")),
        *res,
    )


def finish_kernel(units, gt, vec, g_tok, g_qkv, g_out, g_up, g_down, *vectors):
    l = pl.program_id(0)
    R, D = g_out.shape[1:]
    n_ffn = g_up.shape[2] // D
    group = D // C
    g_tok[...] = gt[...].astype(jnp.float32)

    def read(n, k, cols=slice(None)):
        return units[0, n, k, :, cols].astype(jnp.float32)

    for rb in range(n_ffn):
        for n in range(group):
            u = rb * group + n
            g_up[0, :, u * C : (u + 1) * C] = read(u, 0)
            g_down[0, rb * R : (rb + 1) * R, n * C : (n + 1) * C] = read(u, 1)
    for i in range(D // 128):
        u = n_ffn * group + i
        for k in range(3):
            half = slice(k % 2 * 128, k % 2 * 128 + 128)
            g_qkv[0, :, k * D + i * 128 : k * D + (i + 1) * 128] = read(u, k // 2, half)
        g_out[0, :, i * 128 : (i + 1) * 128] = read(u, 1, slice(128, 256))
    row = 0
    for ref in vectors:
        for k in range(ref.shape[1] // D):
            ref[pl.ds(l, 1), k * D : (k + 1) * D] = vec[0, row : row + 1, :]
            row += 1


def finish(units, grad_tokens, vec, layers, hidden_units):
    n_units, _, R, _ = units.shape
    parts, piece, D = grad_tokens.shape
    L, FF = layers, hidden_units
    f32 = jnp.float32
    S = jax.ShapeDtypeStruct
    per = n_units // L
    widths = (D, D, D, D, D, FF, D, D, D)
    return pl.pallas_call(
        finish_kernel,
        grid=(L,),
        out_shape=(
            S((parts, piece, D), f32), S((L, R, 3 * D), f32), S((L, R, D), f32), S((L, R, FF), f32),
            S((L, FF // WAYS, D), f32),
        ) + tuple(S((L, width), f32) for width in widths),
        in_specs=[
            pl.BlockSpec((1, per, 2, R, C), lambda l: (L - 1 - l, 0, 0, 0, 0)),
            pl.BlockSpec((parts // L, piece, D), lambda l: (l, 0, 0)),
            pl.BlockSpec((1, VEC_ROWS, D), lambda l: (l, 0, 0)),
        ],
        out_specs=(
            pl.BlockSpec((parts // L, piece, D), lambda l: (l, 0, 0)),
            pl.BlockSpec((1, R, 3 * D), lambda l: (l, 0, 0)),
            pl.BlockSpec((1, R, D), lambda l: (l, 0, 0)),
            pl.BlockSpec((1, R, FF), lambda l: (l, 0, 0)),
            pl.BlockSpec((1, FF // WAYS, D), lambda l: (l, 0, 0)),
        ) + tuple(pl.BlockSpec((L, width), lambda l: (0, 0)) for width in widths),
        compiler_params=pltpu.CompilerParams(vmem_limit_bytes=60 * 1024 * 1024),
        name="finish",
    )(units.reshape(L, per, 2, R, C), grad_tokens, vec)


NAMES = (
    "w_qkv",
    "b_query",
    "b_value",
    "w_out",
    "b_out",
    "gain_one",
    "shift_one",
    "w_up",
    "b_up",
    "w_down",
    "b_down",
    "gain_two",
    "shift_two",
)


def by_class(array, block, ways):
    layers, rows, tokens_here = array.shape
    if ways == 1:
        return array.reshape(layers, WAYS, -1, tokens_here)
    array = array.reshape(layers, ways, WAYS, block, tokens_here)
    return jnp.swapaxes(array, 1, 2).reshape(layers, WAYS, -1, tokens_here)


def on_device(dp_count, tokens, segment_ids, pair_ids, *weights):
    w = dict(zip(NAMES, weights))
    layer_count, model_width, _ = w["w_qkv"].shape
    hidden_units = w["w_up"].shape[2]
    ways = dp_count // WAYS
    grad_hidden, loss_value, *res = forward(tokens, segment_ids, pair_ids, w)
    for place in (4, 5, 6):
        res[place] = by_class(res[place], model_width // dp_count, ways)
    block = model_width // WAYS
    acts = by_class(res[7], hidden_units // dp_count, ways)
    res[7] = acts.reshape(layer_count, WAYS, -1, block, acts.shape[-1])
    units, grad_tokens, vec = backward(grad_hidden, res, w)
    if ways > 1:
        groups = [[low + WAYS * high for high in range(ways)] for low in range(WAYS)]
        vec = lax.psum(vec, "dp", axis_index_groups=groups)
    grad_tokens, *rest = finish(units, grad_tokens, vec, layer_count, hidden_units)
    matrices, vectors = rest[:4], rest[4:]
    if ways > 1:
        matrices = [
            lax.psum_scatter(
                matrix, "dp", scatter_dimension=1, axis_index_groups=groups, tiled=True
            )
            for matrix in matrices
        ]
    g_qkv, g_out, g_up, g_down = matrices
    return (
        loss_value.reshape(1),
        grad_tokens,
        g_qkv,
        vectors[0],
        vectors[1],
        g_out,
        vectors[2],
        vectors[3],
        vectors[4],
        g_up,
        vectors[5],
        g_down,
        vectors[6],
        vectors[7],
        vectors[8],
    )


def solution(mesh):
    return jax.shard_map(
        functools.partial(on_device, mesh.shape["dp"]),
        mesh=mesh,
        in_specs=(P("dp", "seq", None), P("dp", "seq"), P("dp")) + (P(),) * 13,
        out_specs=(
            P("dp"),
            P("dp", "seq", None),
            P(None, "dp", None),
            P(),
            P(),
            P(None, "dp", None),
            P(),
            P(),
            P(),
            P(None, "dp", None),
            P(),
            P(None, "dp", None),
            P(),
            P(),
            P(),
        ),
        check_vma=False,
    )
```

profile of v0, /device:TPU:0, one launch (start us, length us, event | category | flops | bytes accessed | tf_op | source)
XLA Modules:
  0.0 229.8 jit_solution(9252865298587042088)
XLA Ops:
  0.6 70.5 %forward.1 = (f32[512,768]{1,0:T(8,128)}, f32[1,1]{1,0:T(1,128)}, bf16[2,512,2304]{2,1,0:T(8,128)(2,1)}, bf16[2,12,512,512]{3,2,1,0:T(8,128)(2,1)}, f32[2,512,76...) custom-call(bf16[4,128,768]{2,1,0:T(8,128)(2,1)} %tok.1, ...), custom_call_target="tpu_custom_call" | custom-call | tf_op jit(solution)/shard_map/forward/pallas_call | solution.py:361
  71.1 151.5 %backward.1 = (bf16[36,2,96,256]{3,2,1,0:T(8,128)(2,1)}, bf16[4,128,768]{2,1,0:T(8,128)(2,1)}, f32[2,16,768]{2,1,0:T(8,128)}) custom-call(f32[512,768]{1,0:T(8,128)} %get-tuple-element.48.g_in, f32[2,768]{1,0:T(2,128)} %gain_one.3, f32[2,768]{1,0:T(2,128)} %gain_two.3, bf16[2,768,2304]{2,1,0:T(8,128)(2,1)} %w_qkv.3, bf16[2,768,768]{2,1,0:T(8,128)(2,1)} %w_out.3, ...), custom_call_target="tpu_custom_call" | custom-call | tf_op jit(solution)/shard_map/backward/pallas_call | solution.py:870
  222.7 5.2 %finish.1 = (f32[4,128,768]{2,1,0:T(8,128)}, f32[2,96,2304]{2,1,0:T(8,128)}, f32[2,96,768]{2,1,0:T(8,128)}, f32[2,96,3072]{2,1,0:T(8,128)}, f32[2,384,768]{2,1,0...) custom-call(bf16[2,18,2,96,256]{4,3,2,1,0:T(8,128)(2,1)} %bitcast.9,, ...), custom_call_target="tpu_custom_call" | custom-call | tf_op jit(solution)/shard_map/finish/pallas_call | solution.py:925
where the time goes:
time: 230 us
  Pallas kernels  227 us (99%)
  between operations  2.48 us (1%)
    pallas_call x1, Pallas kernels, backward(): pl.pallas_call(functools.partial(bwd_kernel, L), out_shape=(S((n_units, 2...  152 us
    pallas_call x1, Pallas kernels, forward(): pl.pallas_call(functools.partial(fwd_kernel, L, segs), out_shape=out_shap...  70.5 us
    pallas_call x1, Pallas kernels, finish(): pl.pallas_call(finish_kernel, grid=(L,), out_shape=(S((parts, piece, D),...  5.24 us

commit v1 on v0

--- a/solution.py
+++ b/solution.py
@@ -15,10 +15,12 @@
 C = 256
 WAYS = 8
 QUEUE = 18
+SLOTS_ONE = 7
 SLOTS = 6
-LAGS = (0, 1, 3, 5, 7, 9, 11)
+LAGS = (0, 1, 4, 6, 8, 10, 12)
 PACE = (5, 6)
 GT_PARTS = 4
+EARLY = 2
 VEC_ROWS = 16
 
 
@@ -60,7 +62,10 @@
     barrier = pltpu.get_barrier_semaphore()
     for peer in peers:
         pl.semaphore_signal(barrier, inc=1, device_id=peer, device_id_type=MESH)
-    pl.semaphore_wait(barrier, len(peers))
+
+
+def await_greetings(peers):
+    pl.semaphore_wait(pltpu.get_barrier_semaphore(), len(peers))
 
 
 def gelu_pair(x):
@@ -113,7 +118,9 @@
             return pltpu.make_async_copy(src.at[zi], dst, tsem.at[n, 0, 0])
         return remote(src.at[peer(k)], dst, tsem.at[n, 0, k], tsem.at[n, 1, k], (me, peer(k)))
 
-    greet([(me, peer(k)) for k in range(1, parts)])
+    peers = [(me, peer(k)) for k in range(1, parts)]
+    greet(peers)
+    await_greetings(peers)
     for k in (2, 1, 3, 0):
         for n in (1, 0):
             tcopy(k, n).start()
@@ -385,9 +392,10 @@
     h_qkv, h_p, h_rl, h_pv, h_hidT, h_mixT, h_nrmT, h_actT, h_gp, h_n1, h_r1, h_n2, h_r2,
     out, gt_out, vec_out,
     wd, wu, gp, actT, wq, qkv, pb, rl, pv, wo, hidT, mixT, nrmT, n1, r1, n2, r2,
-    acc, second, branch, gm, gpre, rhs, vec, vrecv, gb,
+    acc, second, gm, rhs, vec, vlow, vrecv,
     sendc, keepq, recvq, s1, k1, t1, s2, k2, t2, za, zr, zb, zt, zf,
-    fsem, asem, lsem, csem, xsem, ysem, zsem, osem, vsem, gsem,
+    zq, zin, e1, h1, f1, e2, h2, f2, ef, qsem, esem, gather,
+    fsem, asem, lsem, csem, dsem, xsem, ysem, zsem, osem, vsem, gsem,
 ):
     T, D = g_in.shape
     FF = w_up.shape[2]
@@ -399,6 +407,7 @@
     macros = n_ffn + n_att
     per = n_ffn * group + n_att
     n_units = layers * per
+    n_main = n_units - EARLY
     n_macros = layers * macros
 
     me = lax.axis_index("dp")
@@ -455,6 +464,9 @@
         parts = [(h_n1.at[l], n1), (h_r1.at[l], r1), (w_out.at[l], wo)]
         return copies(parts + turned(h_hidT, hidT, l) + turned(h_mixT, mixT, l), lsem.at[1])
 
+    peers = [core, xdev, ydev] + [(me, lax.rem(zi + k, 4)) for k in range(1, 4)]
+    greet(peers)
+
     def start(made):
         for c in made:
             c.start()
@@ -471,7 +483,6 @@
         start(att_tile(jnp.int32(n)))
     acc[...] = g_in[...]
     vec[...] = jnp.zeros_like(vec)
-    greet([core, xdev, ydev] + [(me, lax.rem(zi + k, 4)) for k in range(1, 4)])
 
     lane = lax.broadcasted_iota(jnp.int32, (T, 128), 1)
     first = lane < HD
@@ -482,6 +493,8 @@
 
     def col_sum(v):
         return jnp.sum(v.astype(jnp.float32), axis=0, keepdims=True)
+
+    branch, gpre = second, gm
 
     def through_norm(l, base, normal, root, gain, rounded):
         g = acc[...]
@@ -502,7 +515,7 @@
         through_norm(l, 2, n1, r1, gain_one[pl.ds(l, 1), :], branch)
         gm[...] = dot_t(branch[...], wo[...]).astype(jnp.bfloat16)
 
-    def ffn(l, rb, c):
+    def ffn(l, rb, c, send=None):
         f = (layers - 1 - l) * n_ffn + rb
         s = lax.rem(f, 2)
         q = rb * group
@@ -515,6 +528,8 @@
             for n in range(group):
                 keepq[q + n, k] = made[:U, n * C : (n + 1) * C]
                 sendc[c, n, k] = made[U:, n * C : (n + 1) * C]
+        if send is not None:
+            send()
         acc[...] += dot_t(gpre[...], wu[s])
 
         @pl.when(f + 2 < layers * n_ffn)
@@ -575,11 +590,17 @@
             sendc.at[c, pl.ds(0, size)], recvq.at[pl.ds(q, size)], csem.at[0, m], csem.at[1, m], core
         )
 
+    def first_copy(n):
+        return remote(sendc.at[0, n], recvq.at[n], dsem.at[0, n], dsem.at[1, n], core)
+
     def is_wide(m):
         return lax.rem(m, macros) < n_ffn
 
+    def unit_of(v):
+        return v + jnp.minimum(lax.div(v, 2), EARLY)
+
     def copies_one(u):
-        s = lax.rem(u, SLOTS)
+        s = lax.rem(u, SLOTS_ONE)
         return [
             remote(s1.at[s, k], t1.at[s, k], xsem.at[0, k, s], xsem.at[1, k, s], (xdev, ydev)[k]) for k in range(2)
         ]
@@ -598,24 +619,24 @@
 
     def copy_out(u, k):
         s = lax.rem(u, SLOTS)
-        return remote(zf.at[s, k], out.at[u, k], zsem.at[4, k, s], zsem.at[5, k, s], to_outer)
+        return remote(zf.at[s, k], out.at[unit_of(u), k], zsem.at[4, k, s], zsem.at[5, k, s], to_outer)
 
     def copy_home(u):
         s = lax.rem(u, SLOTS)
-        return pltpu.make_async_copy(zf.at[s], out.at[u], osem.at[s])
-
-    def stage_one(u):
+        return pltpu.make_async_copy(zf.at[s], out.at[unit_of(u)], osem.at[s])
+
+    def stage_one(v):
+        u = unit_of(v)
         s = lax.rem(u, QUEUE)
-        d = lax.rem(u, SLOTS)
-        base = lax.div(u, per) * macros
-
-        @pl.when(u == 0)
-        def _():
-            core_copy(base, True).wait_recv()
-
-        @pl.when(u >= n_units - 2)
-        def _():
-            core_copy(base + n_ffn + s - n_ffn * group, False).wait_recv()
+        d = lax.rem(v, SLOTS_ONE)
+
+        @pl.when(u < group)
+        def _():
+            first_copy(u).wait_recv()
+
+        @pl.when(u == n_units - 1)
+        def _():
+            core_copy(jnp.int32(n_macros - 1), False).wait_recv()
 
         for k in range(2):
             sent, kept = ((1, 3), (0, 2)) if k == 0 else ((2, 3), (0, 1))
@@ -623,14 +644,15 @@
                 to = pl.ds(n * R, R)
                 s1[d, k, to] = low_sum(keepq[s, k, pl.ds(a * R, R)], recvq[s, k, pl.ds(a * R, R)])
                 k1[d, k, to] = low_sum(keepq[s, k, pl.ds(b * R, R)], recvq[s, k, pl.ds(b * R, R)])
-        start(copies_one(u))
+        start(copies_one(v))
 
     def stage_two(u):
-        d = lax.rem(u, SLOTS)
+        d = lax.rem(u, SLOTS_ONE)
+        e = lax.rem(u, SLOTS)
         wait(copies_one(u))
         for k in range(2):
-            s2[d, k] = low_sum(k1[d, k, pl.ds(R, R)], t1[d, k, pl.ds(R, R)])
-            k2[d, k] = low_sum(k1[d, k, pl.ds(0, R)], t1[d, k, pl.ds(0, R)])
+            s2[e, k] = low_sum(k1[d, k, pl.ds(R, R)], t1[d, k, pl.ds(R, R)])
+            k2[e, k] = low_sum(k1[d, k, pl.ds(0, R)], t1[d, k, pl.ds(0, R)])
         start([copy_two(u, k) for k in range(2)])
 
     def stage_three(u):
@@ -686,18 +708,89 @@
     def run_stage(i, k):
         u = i - LAGS[k]
 
-        @pl.when((u >= 0) & (u < n_units))
+        @pl.when((u >= 0) & (u < n_main))
         def _():
             stages[k](u)
+
+    def quarter_copy(n, d):
+        peer = lax.rem(zi + d, 4)
+        return remote(
+            zq.at[n, peer], zin.at[n, d - 1], qsem.at[0, n, d - 1], qsem.at[1, n, d - 1], (me, peer)
+        )
+
+    def early_one(n):
+        return remote(e1.at[n], f1.at[n], esem.at[0, n], esem.at[1, n], (xdev, ydev)[n % 2])
+
+    def early_two(n):
+        return remote(e2.at[n], f2.at[n], esem.at[2, n], esem.at[3, n], (ydev, xdev)[n % 2])
+
+    def early_place(n):
+        half = pl.ds(pl.multiple_of(lax.rem(zi, 2) * 128, 128), 128)
+        return out.at[group * n + group - 1, lax.div(zi, 2), :, half]
+
+    def early_out(n, d):
+        peer = lax.rem(zi + d, 4)
+        return remote(ef.at[n], early_place(n), gather.at[0, n, d], gather.at[1, n, d], (me, peer))
+
+    def early_home(n):
+        return pltpu.make_async_copy(ef.at[n], early_place(n), gather.at[0, n, 0])
+
+    def early_steps(i, n):
+        u = group * n + group - 1
+
+        @pl.when(i == 1 + 2 * n)
+        def _():
+            if n == 0:
+                first_copy(u).wait_recv()
+            for k in range(2):
+                made = low_sum(keepq[u, k], recvq[u, k])
+                for h in range(2):
+                    zq[n, 2 * k + h] = made[:, h * 128 : (h + 1) * 128]
+            for d in (2, 1, 3):
+                quarter_copy(n, d).start()
+
+        @pl.when(i == 10 + 2 * n)
+        def _():
+            for d in range(1, 4):
+                quarter_copy(n, d).wait()
+            made = zq[n, zi].astype(jnp.float32)
+            for d in range(3):
+                made = made + zin[n, d].astype(jnp.float32)
+            made = made.astype(jnp.bfloat16)
+            sent, kept = ((1, 3), (0, 2)) if n % 2 == 0 else ((2, 3), (0, 1))
+            for j in range(2):
+                e1[n, j * R : (j + 1) * R] = made[sent[j] * R : (sent[j] + 1) * R]
+                h1[n, j * R : (j + 1) * R] = made[kept[j] * R : (kept[j] + 1) * R]
+
+        @pl.when(i == n_main + 1)
+        def _():
+            early_one(n).start()
+
+        @pl.when(i == n_main + 5)
+        def _():
+            early_one(n).wait()
+            e2[n] = low_sum(h1[n, R:], f1[n, R:])
+            h2[n] = low_sum(h1[n, :R], f1[n, :R])
+            early_two(n).start()
+
+        @pl.when(i == n_main + 9)
+        def _():
+            early_two(n).wait()
+            ef[n] = low_sum(h2[n], f2[n])
+            for d in range(1, 4):
+                early_out(n, d).start()
+            early_home(n).start()
 
     def vec_copy(k):
         where = (core, xdev, ydev, to_inner, across, to_outer)[k]
-        return remote(vec, vrecv.at[k], vsem.at[0, k], vsem.at[1, k], where)
+        return remote(vlow, vrecv.at[k], vsem.at[0, k], vsem.at[1, k], where)
 
     def vec_step(k):
         if 1 <= k <= 3:
             vec_copy(k - 1).wait()
-            vec[...] += vrecv[k - 1]
+            vlow[...] += vrecv[k - 1]
+        if k == 0:
+            vlow[...] = vec[...].astype(jnp.bfloat16)
         if k < 3:
             vec_copy(k).start()
         if k == 3:
@@ -715,7 +808,7 @@
             @pl.when(inner)
             def _():
                 vec_copy(3).wait_recv()
-                vec[...] += vrecv[3]
+                vlow[...] += vrecv[3]
                 vec_copy(4).start()
 
         if k == 5:
@@ -723,7 +816,7 @@
             @pl.when(inner)
             def _():
                 vec_copy(4).wait()
-                vec[...] += vrecv[4]
+                vlow[...] += vrecv[4]
                 vec_copy(5).start()
 
         if k == 6:
@@ -731,24 +824,24 @@
             @pl.when(inner)
             def _():
                 vec_copy(5).wait_send()
-                vec_out[...] = vec[...]
+                vec_out[...] = vlow[...].astype(jnp.float32)
 
             @pl.when(outer)
             def _():
                 vec_copy(5).wait_recv()
-                vec_out[...] = vrecv[5]
+                vec_out[...] = vrecv[5].astype(jnp.float32)
 
     part = T // 4
     slab = part // GT_PARTS
 
     def gt_own():
         own = pl.ds(pl.multiple_of(zi * part, part), part)
-        return pltpu.make_async_copy(gb.at[own], gt_out.at[zi], gsem.at[0, 3 * GT_PARTS])
+        return pltpu.make_async_copy(gm.at[own], gt_out.at[zi], gsem.at[0, 3 * GT_PARTS])
 
     def gt_copy(n):
         peer = lax.rem(zi + 1 + lax.rem(n, 3), 4)
         o = lax.div(n, 3) * slab
-        src = gb.at[pl.ds(pl.multiple_of(peer * part + o, slab), slab)]
+        src = gm.at[pl.ds(pl.multiple_of(peer * part + o, slab), slab)]
         dst = gt_out.at[zi, pl.ds(pl.multiple_of(o, slab), slab)]
         return remote(src, dst, gsem.at[0, n], gsem.at[1, n], (me, peer))
 
@@ -768,19 +861,20 @@
         l = layers - 1 - lax.div(m, macros)
         k = lax.rem(m, macros)
         c = lax.rem(m, 2)
-        busy = done_by(i) > m
-
-        @pl.when(busy & (m >= 2) & is_wide(m - 2))
+        busy = (done_by(i) > m) & (m > 0)
+
+        @pl.when(busy & (m == 2))
+        def _():
+            for n in range(group):
+                first_copy(n).wait_send()
+
+        @pl.when(busy & (m >= 3) & is_wide(m - 2))
         def _():
             core_copy(m - 2, True).wait_send()
 
-        @pl.when(busy & (m >= 3) & is_wide(m - 2))
-        def _():
-            core_copy(m - 2, True).wait_recv()
-
         @pl.when(busy & (m >= 2) & ~is_wide(m - 2))
         def _():
-            core_copy(m - 2, False).wait()
+            core_copy(m - 2, False).wait_send()
 
         @pl.when(busy & (k == 0))
         def _():
@@ -793,24 +887,41 @@
         @pl.when(busy & (k < n_ffn))
         def _():
             ffn(l, k, c)
+
+        @pl.when(busy & (k == n_ffn) & (l > 0))
+        def _():
+            start(ffn_layer(l - 1))
+
+        @pl.when(busy & (k == n_ffn))
+        def _():
+            middle(l)
+
+        @pl.when(busy & (k >= n_ffn))
+        def _():
+            attend(l, k - n_ffn, c)
+
+        @pl.when(busy & (m >= 2) & is_wide(m - 1))
+        def _():
+            core_copy(m - 1, True).wait_recv()
+
+        @pl.when(busy & (m >= 2) & ~is_wide(m - 1))
+        def _():
+            core_copy(m - 1, False).wait_recv()
+
+        @pl.when(busy & (k < n_ffn))
+        def _():
             core_copy(m, True).start()
 
-        @pl.when(busy & (k == n_ffn) & (l > 0))
-        def _():
-            start(ffn_layer(l - 1))
-
-        @pl.when(busy & (k == n_ffn))
-        def _():
-            middle(l)
-
         @pl.when(busy & (k >= n_ffn))
         def _():
-            attend(l, k - n_ffn, c)
             core_copy(m, False).start()
 
+        for n in range(EARLY):
+            early_steps(i, n)
+
         @pl.when(i == last + 1)
         def _():
-            gb[...] = acc[...].astype(jnp.bfloat16)
+            gm[...] = acc[...].astype(jnp.bfloat16)
             gt_own().start()
 
         @pl.when((i > last) & (i <= last + 3 * GT_PARTS))
@@ -825,7 +936,18 @@
 
         return carry
 
-    lax.fori_loop(0, n_units + LAGS[6], step, 0)
+    def first_sends():
+        await_greetings(peers)
+        for n in range(group):
+            first_copy(n).start()
+
+    prologue(layers - 1)
+    ffn(layers - 1, jnp.int32(0), 0, first_sends)
+    lax.fori_loop(1, n_main + LAGS[6], step, 0)
+    for n in range(EARLY):
+        early_home(n).wait()
+        for d in range(1, 4):
+            early_out(n, d).wait()
     for m in (n_macros - 2, n_macros - 1):
         core_copy(jnp.int32(m), False).wait_send()
     gt_own().wait()
@@ -857,14 +979,18 @@
         V((2, D, 384), bf), V((2, T, 384), bf), V((2, 2, T, T), bf), V((2, T, 128), f32), V((2, T, 128), f32),
         V((D, D), bf), V((D, T), bf), V((D, T), bf), V((D, T), bf),
         V((T, D), bf), V((T, 128), f32), V((T, D), bf), V((T, 128), f32),
-        V((T, D), f32), V((T, D), bf), V((T, D), bf), V((T, D), bf), V((T, D), bf), V((T, 384), bf),
-        V((L, VEC_ROWS, D), f32), V((6, L, VEC_ROWS, D), f32), V((T, D), bf),
+        V((T, D), f32), V((T, D), bf), V((T, D), bf), V((T, 384), bf),
+        V((L, VEC_ROWS, D), f32), V((L, VEC_ROWS, D), bf), V((6, L, VEC_ROWS, D), bf),
         V((2, group, 2, U, C), bf), V((QUEUE, 2, U, C), bf), V((QUEUE, 2, U, C), bf),
-        V((SLOTS, 2, 2 * R, C), bf), V((SLOTS, 2, 2 * R, C), bf), V((SLOTS, 2, 2 * R, C), bf),
+        V((SLOTS_ONE, 2, 2 * R, C), bf), V((SLOTS_ONE, 2, 2 * R, C), bf), V((SLOTS_ONE, 2, 2 * R, C), bf),
         V((SLOTS, 2, R, C), bf), V((SLOTS, 2, R, C), bf), V((SLOTS, 2, R, C), bf),
         V((SLOTS, 2, R, C), bf), V((SLOTS, 2, R, C), bf), V((SLOTS, 2, R, C), bf),
         V((SLOTS, 2, R, C), bf), V((SLOTS, 2, R, C), bf),
-        dma((2, 3 + WAYS)), dma((2, 9)), dma((2, 3 + 2 * WAYS)), dma((2, n_macros)), dma((2, 2, SLOTS)), dma((2, 2, SLOTS)),
+        V((EARLY, 4, U, 128), bf), V((EARLY, 3, U, 128), bf),
+        V((EARLY, 2 * R, 128), bf), V((EARLY, 2 * R, 128), bf), V((EARLY, 2 * R, 128), bf),
+        V((EARLY, R, 128), bf), V((EARLY, R, 128), bf), V((EARLY, R, 128), bf), V((EARLY, R, 128), bf),
+        dma((2, EARLY, 3)), dma((4, EARLY)), dma((2, EARLY, 4)),
+        dma((2, 3 + WAYS)), dma((2, 9)), dma((2, 3 + 2 * WAYS)), dma((2, n_macros)), dma((2, group)), dma((2, 2, SLOTS_ONE)), dma((2, 2, SLOTS)),
         dma((6, 2, SLOTS)), dma((SLOTS,)), dma((2, 6)), dma((2, 3 * GT_PARTS + 1)),
     ]
     return pl.pallas_call(

time: 230 us -> 227 us (0.987)
  Pallas kernels: 227 us -> 224 us
    pallas_call x1, Pallas kernels: 152 us -> 148 us  [backward(): pl.pallas_call(functools.partial(bwd_kernel, L), out_shape=(S((n_units, 2...]
where the time goes in v1:
time: 227 us; the launch traced here: 226 us
  Pallas kernels  224 us (99%)
  between operations  2.48 us (1%)
    pallas_call x1, Pallas kernels, backward(): pl.pallas_call(functools.partial(bwd_kernel, L), out_shape=(S((n_units, 2...  148 us
    pallas_call x1, Pallas kernels, forward(): pl.pallas_call(functools.partial(fwd_kernel, L, segs), out_shape=out_shap...  70.5 us
    pallas_call x1, Pallas kernels, finish(): pl.pallas_call(finish_kernel, grid=(L,), out_shape=(S((parts, piece, D),...  5.24 us

profile of v1, /device:TPU:0, one launch (start us, length us, event | category | flops | bytes accessed | tf_op | source)
XLA Modules:
  0.0 226.4 jit_solution(9587981957046875636)
XLA Ops:
  0.6 70.5 %forward.1 = (f32[512,768]{1,0:T(8,128)}, f32[1,1]{1,0:T(1,128)}, bf16[2,512,2304]{2,1,0:T(8,128)(2,1)}, bf16[2,12,512,512]{3,2,1,0:T(8,128)(2,1)}, f32[2,512,76...) custom-call(bf16[4,128,768]{2,1,0:T(8,128)(2,1)} %tok.1, ...), custom_call_target="tpu_custom_call" | custom-call | tf_op jit(solution)/shard_map/forward/pallas_call | solution.py:368
  71.1 148.2 %backward.1 = (bf16[36,2,96,256]{3,2,1,0:T(8,128)(2,1)}, bf16[4,128,768]{2,1,0:T(8,128)(2,1)}, f32[2,16,768]{2,1,0:T(8,128)}) custom-call(f32[512,768]{1,0:T(8,128)} %get-tuple-element.48.g_in, f32[2,768]{1,0:T(2,128)} %gain_one.3, f32[2,768]{1,0:T(2,128)} %gain_two.3, bf16[2,768,2304]{2,1,0:T(8,128)(2,1)} %w_qkv.3, bf16[2,768,768]{2,1,0:T(8,128)(2,1)} %w_out.3, ...), custom_call_target="tpu_custom_call" | custom-call | tf_op jit(solution)/shard_map/backward/pallas_call | solution.py:996
  219.3 5.2 %finish.1 = (f32[4,128,768]{2,1,0:T(8,128)}, f32[2,96,2304]{2,1,0:T(8,128)}, f32[2,96,768]{2,1,0:T(8,128)}, f32[2,96,3072]{2,1,0:T(8,128)}, f32[2,384,768]{2,1,0...) custom-call(bf16[2,18,2,96,256]{4,3,2,1,0:T(8,128)(2,1)} %bitcast.9,, ...), custom_call_target="tpu_custom_call" | custom-call | tf_op jit(solution)/shard_map/finish/pallas_call | solution.py:1051

commit v2 on v1

--- a/solution.py
+++ b/solution.py
@@ -475,13 +475,10 @@
         for c in made:
             c.wait()
 
+    arriving = pltpu.make_async_copy(g_in, acc, lsem.at[0, 2 + 2 * WAYS])
+    arriving.start()
     start(ffn_layer(layers - 1))
-    for n in range(2):
-        start(ffn_tile(jnp.int32(n)))
-    start(att_layer(layers - 1))
-    for n in range(2):
-        start(att_tile(jnp.int32(n)))
-    acc[...] = g_in[...]
+    start(ffn_tile(jnp.int32(0)))
     vec[...] = jnp.zeros_like(vec)
 
     lane = lax.broadcasted_iota(jnp.int32, (T, 128), 1)
@@ -941,7 +938,12 @@
         for n in range(group):
             first_copy(n).start()
 
+    arriving.wait()
     prologue(layers - 1)
+    start(ffn_tile(jnp.int32(1)))
+    start(att_layer(layers - 1))
+    for n in range(2):
+        start(att_tile(jnp.int32(n)))
     ffn(layers - 1, jnp.int32(0), 0, first_sends)
     lax.fori_loop(1, n_main + LAGS[6], step, 0)
     for n in range(EARLY):
@@ -998,7 +1000,7 @@
         out_shape=(
             S((n_units, 2, R, C), bf), S((4, T // 4, D), bf), S((L, VEC_ROWS, D), f32),
         ),
-        in_specs=[vm] * 3 + [anyspec] * 17,
+        in_specs=[anyspec] + [vm] * 2 + [anyspec] * 17,
         out_specs=(anyspec, anyspec, vm),
         scratch_shapes=scratch,
         compiler_params=pltpu.CompilerParams(

time: 227 us -> 226 us (level)
  no operation moved by 1% of the time
where the time goes in v2:
time: 226 us
  Pallas kernels  223 us (99%)
  between operations  2.48 us (1%)
    pallas_call x1, Pallas kernels, backward(): pl.pallas_call(functools.partial(bwd_kernel, L), out_shape=(S((n_units, 2...  147 us
    pallas_call x1, Pallas kernels, forward(): pl.pallas_call(functools.partial(fwd_kernel, L, segs), out_shape=out_shap...  70.5 us
    pallas_call x1, Pallas kernels, finish(): pl.pallas_call(finish_kernel, grid=(L,), out_shape=(S((parts, piece, D),...  5.24 us

profile of v2, /device:TPU:0, one launch (start us, length us, event | category | flops | bytes accessed | tf_op | source)
XLA Modules:
  0.0 225.5 jit_solution(13786628608958068037)
XLA Ops:
  0.6 70.5 %forward.1 = (f32[512,768]{1,0:T(8,128)}, f32[1,1]{1,0:T(1,128)}, bf16[2,512,2304]{2,1,0:T(8,128)(2,1)}, bf16[2,12,512,512]{3,2,1,0:T(8,128)(2,1)}, f32[2,512,76...) custom-call(bf16[4,128,768]{2,1,0:T(8,128)(2,1)} %tok.1, ...), custom_call_target="tpu_custom_call" | custom-call | tf_op jit(solution)/shard_map/forward/pallas_call | solution.py:368
  71.1 147.3 %backward.1 = (bf16[36,2,96,256]{3,2,1,0:T(8,128)(2,1)}, bf16[4,128,768]{2,1,0:T(8,128)(2,1)}, f32[2,16,768]{2,1,0:T(8,128)}) custom-call(f32[512,768]{1,0:T(8,128)} %get-tuple-element.48.g_in, f32[2,768]{1,0:T(2,128)} %gain_one.3, f32[2,768]{1,0:T(2,128)} %gain_two.3, bf16[2,768,2304]{2,1,0:T(8,128)(2,1)} %w_qkv.3, bf16[2,768,768]{2,1,0:T(8,128)(2,1)} %w_out.3, ...), custom_call_target="tpu_custom_call" | custom-call | tf_op jit(solution)/shard_map/backward/pallas_call | solution.py:998
  218.5 5.2 %finish.1 = (f32[4,128,768]{2,1,0:T(8,128)}, f32[2,96,2304]{2,1,0:T(8,128)}, f32[2,96,768]{2,1,0:T(8,128)}, f32[2,96,3072]{2,1,0:T(8,128)}, f32[2,384,768]{2,1,0...) custom-call(bf16[2,18,2,96,256]{4,3,2,1,0:T(8,128)(2,1)} %bitcast.9,, ...), custom_call_target="tpu_custom_call" | custom-call | tf_op jit(solution)/shard_map/finish/pallas_call | solution.py:1053
